TPU v7x, 32 devices: a whole 2x2x4 slice. The times are simulated.
32 devices in a mesh: dp: 8 (over y, x, core), blk: 4 (over z).
Axes of the slice: x: 2, y: 2, z: 4, core: 2. Of those that a mesh axis runs over, the one named last changes fastest.
Arguments:
- prod_feat: bfloat16 [8, 3072, 768], P('dp', 'blk'), may hold values from -23 to 23
- prec_feat: bfloat16 [8, 3072, 768], P('dp', 'blk'), may hold values from -23 to 23
- matched: int32 [8, 3072], P('dp', 'blk'), may hold values from 0 to 3071, each once within a row
- row_weight: float32 [8, 3072], P('dp', 'blk'), may hold values from 0.2 to 28, as said below
- proj_prod: bfloat16 [768, 1024], replicated, may hold values from -0.21875 to 0.21875
- proj_prec: bfloat16 [768, 1024], replicated, may hold values from -0.21875 to 0.21875
Outputs:
- loss_value: float32 [], replicated
- grad_prod: float32 [768, 1024], P('dp', 'blk')
- grad_prec: float32 [768, 1024], P('dp', 'blk')
Inputs may be any that keep to these rules, and one draw needn't show every extreme that they name: `matched`: in each of the 8 groups the 3072 values are a permutation of 0 to 3071. `row_weight`: positive.
All inputs are finite; a program needn't handle non-finite values.
Results may differ from a plain program's by a relative error of at most 0.0027.
Values may be sent and summed in bfloat16 or wider, within the bound.
A program may use at most 128 MiB of HBM per device.

v0:
```python
import functools
import math

import jax
import jax.numpy as jnp
from jax import lax
from jax.experimental import pallas as pl
from jax.experimental.pallas import tpu as pltpu
from jax.sharding import PartitionSpec as P

EPS = 1e-06
LOGIT_SCALE = 50.0
MESH = pl.DeviceIdType.MESH
F32 = jnp.float32
BF16 = jnp.bfloat16


def embed_rows(features, weight):
    raw = jnp.dot(features, weight, preferred_element_type=F32)
    radius = jnp.sqrt(jnp.sum(raw * raw, axis=1, keepdims=True) + EPS)
    unit = raw / radius
    return unit, unit.astype(BF16), radius


def backward_kernel(
    nx, ny, nz,
    s00, s01, s10, s11, t00, t01, t10, t11, w0, w1, tot0, tot1, rp0, rp1, rc0, rc1,
    up0, up1, uc0, uc1, fp0, fp1, fc0, fc1, stats_ref,
    oa_ref, ob_ref, stats_out,
    coeffs_t, high, low, head, core_in, first_out, first_in, own, second_out, second_in, last, last_in,
    stats_now, stats_in,
    core_s, core_r, first_s, first_r, second_s, second_r, last_s, last_r, stats_s, stats_r,
):
    dp = lax.axis_index("dp")
    z = lax.axis_index("blk")
    core = lax.rem(dp, 2)
    x = lax.rem(dp // 2, nx)
    y = dp // (2 * nx)

    def at(yy, xx, cc, zz):
        return ((yy * nx + xx) * 2 + cc, zz)

    def along_x(k):
        return at(y, lax.rem(x + k, nx), core, z)

    def along_y(k):
        return at(lax.rem(y + k, ny), x, core, z)

    def along_z(k):
        return at(y, x, core, lax.rem(z + k, nz))

    twin = at(y, x, 1 - core, z)
    axes = [
        [twin],
        [along_x(k) for k in range(1, nx)],
        [along_y(k) for k in range(1, ny)],
        [along_z(k) for k in range(1, nz)],
    ]
    partners = sum(axes, [])
    barrier = pltpu.get_barrier_semaphore()
    for partner in partners:
        pl.semaphore_signal(barrier, inc=1, device_id=partner, device_id_type=MESH)
    pl.semaphore_wait(barrier, len(partners))

    def send(src, dst, s_sem, r_sem, to):
        copy = pltpu.make_async_remote_copy(
            src_ref=src, dst_ref=dst, send_sem=s_sem, recv_sem=r_sem, device_id=to, device_id_type=MESH
        )
        copy.start()
        return copy

    def stats_start(axis):
        return [
            send(stats_now.at[axis], stats_in.at[axis, k], stats_s.at[axis, k], stats_r.at[axis, k], to)
            for k, to in enumerate(axes[axis])
        ]

    def stats_end(axis, copies):
        total = stats_now[axis]
        for k, copy in enumerate(copies):
            copy.wait()
            total = total + stats_in[axis, k]
        return total

    rows, feat = fp0.shape
    cols = up0.shape[1]
    groups = nx * ny
    r = feat // (groups * 2)
    width = cols // nz
    half = width // 2

    n1, n2 = (nx, ny), (ny, nx)
    me1, me2 = (x, y), (y, x)
    to1, to2 = (along_x, along_y), (along_y, along_x)

    def head_rows(g, cc):
        return pl.ds(pl.multiple_of((g * 2 + cc) * r, 8), r)

    def core_start(h):
        return [
            send(head.at[h, head_rows(g, 1 - core)], core_in.at[h, g], core_s.at[h, g], core_r.at[h, g], twin)
            for g in range(groups)
        ]

    def place(q, i1, i2):
        return i2 * nx + i1 if q == 0 else i1 * nx + i2

    def piece(h, q, g, zz):
        columns = slice(zz * width + q * half, zz * width + (q + 1) * half)
        return head[h, head_rows(g, core), columns] + core_in[h, g, :, columns]

    def first_start(h, copies):
        for copy in copies:
            copy.wait()
        started = [[], []]
        for q in range(2):
            p = 2 * h + q
            for k in range(1, n1[q]):
                there = lax.rem(me1[q] + k, n1[q])
                for j in range(n2[q]):
                    for zz in range(nz):
                        first_out[p, k - 1, j, :, zz * half:(zz + 1) * half] = piece(h, q, place(q, there, j), zz).astype(BF16)
                started[q].append(
                    send(first_out.at[p, k - 1], first_in.at[p, k - 1], first_s.at[p, k - 1], first_r.at[p, k - 1], to1[q](k))
                )
        for q in range(2):
            for j in range(n2[q]):
                for zz in range(nz):
                    own[2 * h + q, j, :, zz * half:(zz + 1) * half] = piece(h, q, place(q, me1[q], j), zz)
        return started

    def second_start(h, copies):
        started = [[], []]
        for q in range(2):
            p = 2 * h + q
            for copy in copies[q]:
                copy.wait()

            def summed(j):
                total = own[p, j]
                for m in range(n1[q] - 1):
                    total = total + first_in[p, m, j].astype(F32)
                return total

            for k in range(1, n2[q]):
                second_out[p, k - 1] = summed(lax.rem(me2[q] + k, n2[q])).astype(BF16)
                started[q].append(
                    send(second_out.at[p, k - 1], second_in.at[p, k - 1], second_s.at[p, k - 1], second_r.at[p, k - 1], to2[q](k))
                )
            last[p] = summed(me2[q])
        return started

    def last_start(h, copies):
        started = [[], []]
        for q in range(2):
            p = 2 * h + q
            for copy in copies[q]:
                copy.wait()
            total = last[p]
            for m in range(n2[q] - 1):
                total = total + second_in[p, m].astype(F32)
            last[p] = total
            for k in range(1, nz):
                columns = pl.ds(pl.multiple_of(lax.rem(z + k, nz) * half, half), half)
                started[q].append(
                    send(last.at[p, :, columns], last_in.at[p, k - 1], last_s.at[p, k - 1], last_r.at[p, k - 1], along_z(k))
                )
        return started

    def finish(h, copies, out_ref):
        for q in range(2):
            p = 2 * h + q
            for copy in copies[q]:
                copy.wait()
            total = last[p, :, pl.ds(pl.multiple_of(z * half, half), half)]
            for m in range(nz - 1):
                total = total + last_in[p, m]
            out_ref[:, q * half:(q + 1) * half] = total

    scores = ((s00, s01), (s10, s11))
    relative = ((t00, t01), (t10, t11))
    weights, totals = (w0, w1), (tot0, tot1)
    radius_p, radius_c = (rp0, rp1), (rc0, rc1)
    unit_p, unit_c = (up0, up1), (uc0, uc1)
    feat_p, feat_c = (fp0, fp1), (fc0, fc1)
    step = 256

    def directions(grad, unit, radius, where):
        grad = LOGIT_SCALE * grad
        unit = unit.astype(F32)
        direction = (grad - unit * jnp.sum(unit * grad, axis=1, keepdims=True)) / radius
        top = direction.astype(BF16)
        high[where, :] = top
        low[where, :] = (direction - top.astype(F32)).astype(BF16)

    def prod_side(i):
        def body(b, carry):
            start = pl.multiple_of(b * step, step)
            block = pl.ds(start, step)
            grad = None
            for j in range(2):
                probability = jnp.exp(scores[i][j][block, :] - LOGIT_SCALE) / totals[i][block, :]
                match = relative[i][j][block, :] == lax.broadcasted_iota(jnp.int32, (step, rows), 1)
                coeffs = (weights[i][block, :] * (probability - match.astype(F32))).astype(BF16)
                coeffs_t[i, j * rows:(j + 1) * rows, block] = coeffs.T
                term = jnp.dot(coeffs, unit_c[j][...], preferred_element_type=F32)
                grad = term if grad is None else grad + term
            directions(grad, unit_p[i][block, :], radius_p[i][block, :], pl.ds(i * rows + start, step))
            return carry

        lax.fori_loop(0, rows // step, body, 0)

    def prec_side(j):
        def body(b, carry):
            start = pl.multiple_of(b * step, step)
            block = pl.ds(start, step)
            here = pl.ds(j * rows + start, step)
            grad = jnp.dot(coeffs_t[0, here, :], unit_p[0][...], preferred_element_type=F32)
            grad = grad + jnp.dot(coeffs_t[1, here, :], unit_p[1][...], preferred_element_type=F32)
            directions(grad, unit_c[j][block, :], radius_c[j][block, :], here)
            return carry

        lax.fori_loop(0, rows // step, body, 0)

    def outer(h, features):
        def body(b, carry):
            block = pl.ds(pl.multiple_of(b * step, step), step)
            total = None
            for i in range(2):
                turned = features[i][:, block].T
                for term in (high, low):
                    product = jnp.dot(turned, term[i * rows:(i + 1) * rows, :], preferred_element_type=F32)
                    total = product if total is None else total + product
            head[h, block, :] = total
            return carry

        lax.fori_loop(0, feat // step, body, 0)

    stats_now[0] = stats_ref[...]
    small = stats_start(0)
    prod_side(0)
    prod_side(1)
    stats_now[1] = stats_end(0, small)
    small = stats_start(1)
    outer(0, feat_p)
    core_p = core_start(0)
    prec_side(0)
    first_p = first_start(0, core_p)
    stats_now[2] = stats_end(1, small)
    small = stats_start(2)
    prec_side(1)
    second_p = second_start(0, first_p)
    stats_now[3] = stats_end(2, small)
    small = stats_start(3)
    outer(1, feat_c)
    core_c = core_start(1)
    last_p = last_start(0, second_p)
    first_c = first_start(1, core_c)
    second_c = second_start(1, first_c)
    last_c = last_start(1, second_c)
    finish(0, last_p, oa_ref)
    stats_out[...] = stats_end(3, small)
    finish(1, last_c, ob_ref)


def backward(nx, ny, nz, *operands):
    feat = operands[-2].shape[1]
    rows, cols = operands[16].shape
    groups = nx * ny
    r = feat // (groups * 2)
    half = cols // nz // 2
    n = max(nx, ny)
    most = max(n, nz) - 1
    out = jax.ShapeDtypeStruct((r, cols // nz), F32)
    dma = pltpu.SemaphoreType.DMA
    vmem = pl.BlockSpec(memory_space=pltpu.VMEM)
    return pl.pallas_call(
        functools.partial(backward_kernel, nx, ny, nz),
        out_shape=(out, out, jax.ShapeDtypeStruct((8, 128), F32)),
        in_specs=[vmem] * len(operands),
        out_specs=(vmem,) * 3,
        scratch_shapes=[
            pltpu.VMEM((2, 2 * rows, rows), BF16),
            pltpu.VMEM((2 * rows, cols), BF16),
            pltpu.VMEM((2 * rows, cols), BF16),
            pltpu.VMEM((2, feat, cols), F32),
            pltpu.VMEM((2, groups, r, cols), F32),
            pltpu.VMEM((4, n - 1, n, r, cols // 2), BF16),
            pltpu.VMEM((4, n - 1, n, r, cols // 2), BF16),
            pltpu.VMEM((4, n, r, cols // 2), F32),
            pltpu.VMEM((4, n - 1, r, cols // 2), BF16),
            pltpu.VMEM((4, n - 1, r, cols // 2), BF16),
            pltpu.VMEM((4, r, cols // 2), F32),
            pltpu.VMEM((4, nz - 1, r, half), F32),
            pltpu.VMEM((4, 8, 128), F32),
            pltpu.VMEM((4, most, 8, 128), F32),
            dma((2, groups)), dma((2, groups)),
            dma((4, n - 1)), dma((4, n - 1)),
            dma((4, n - 1)), dma((4, n - 1)),
            dma((4, nz - 1)), dma((4, nz - 1)),
            dma((4, most)), dma((4, most)),
        ],
        compiler_params=pltpu.CompilerParams(
            collective_id=0, has_side_effects=True, vmem_limit_bytes=60 * 1024 * 1024
        ),
        name="backward",
    )(*operands)


def per_device(nx, ny, prod_feat, prec_feat, matched, row_weight, proj_prod, proj_prec):
    n = lax.axis_size("blk")
    z = lax.axis_index("blk")
    side = [(i, i ^ 1) for i in range(n)]
    across = [(i, n - 1 - i) for i in range(n)]
    own_p, own_c, own_t, own_w = prod_feat[0], prec_feat[0], matched[0], row_weight[0]
    rows = own_p.shape[0]
    far_t = lax.ppermute(own_t, "blk", side)
    far_w = lax.ppermute(own_w, "blk", side)
    far_p = lax.ppermute(own_p, "blk", side)
    far_c = lax.ppermute(own_c, "blk", across)

    feat_p, feat_c = (own_p, far_p), (own_c, far_c)
    targets, weights = (own_t, far_t), (own_w, far_w)
    p = [embed_rows(f, proj_prod) for f in feat_p]
    c = [embed_rows(f, proj_prec) for f in feat_c]
    starts = (z * rows, (n - 1 - z) * rows)

    def scores_of(i, j):
        return LOGIT_SCALE * lax.dot_general(
            p[i][1], c[j][1], (((1,), (1,)), ((), ())), preferred_element_type=F32
        )

    scores = [[scores_of(i, j) for j in range(2)] for i in range(2)]
    matches = [
        [targets[i][:, None] == (starts[j] + lax.iota(jnp.int32, rows))[None, :] for j in range(2)] for i in range(2)
    ]
    part = [sum(jnp.sum(jnp.exp(scores[i][j] - LOGIT_SCALE), axis=1) for j in range(2)) for i in range(2)]
    both = jnp.stack([part[1], part[0]])
    both = lax.ppermute(both, "blk", side)
    totals = [part[0] + both[0], part[1] + both[1]]
    positive = [sum(jnp.sum(jnp.where(matches[i][j], scores[i][j], 0.0), axis=1) for j in range(2)) for i in range(2)]
    loss_local = (
        jnp.sum(own_w * (LOGIT_SCALE + jnp.log(totals[0]))) - jnp.sum(own_w * positive[0]) - jnp.sum(far_w * positive[1])
    )
    stats = jnp.where(lax.iota(jnp.int32, 8)[:, None] == 0, loss_local, jnp.sum(own_w)) * jnp.ones((8, 128), F32)
    relative = [(targets[i] - starts[j])[:, None] for i in range(2) for j in range(2)]
    sum_p, sum_c, stats = backward(
        nx, ny, n,
        *scores[0], *scores[1], *relative, *(w[:, None] for w in weights), *(t[:, None] for t in totals),
        p[0][2], p[1][2], c[0][2], c[1][2], p[0][1], p[1][1], c[0][1], c[1][1], *feat_p, *feat_c, stats,
    )
    weight_total = stats[1, 0]
    return (stats[0, 0] / weight_total, sum_p / weight_total, sum_c / weight_total)


def solution(mesh):
    chips = mesh.shape["dp"] // 2
    ny = math.isqrt(chips)
    nx = chips // ny
    placed = (P("dp", "blk", None), P("dp", "blk", None), P("dp", "blk"), P("dp", "blk"), P(), P())
    return jax.shard_map(
        functools.partial(per_device, nx, ny),
        mesh=mesh,
        in_specs=placed,
        out_specs=(P(), P("dp", "blk"), P("dp", "blk")),
        check_vma=False,
    )
```

profile of v0, /device:TPU:0, one launch (start us, length us, event | category | flops | bytes accessed | tf_op | source)
XLA Modules:
  0.0 161.3 jit_solution(6258521736397608463)
XLA Ops:
  0.6 0.0 copy-start
  0.7 0.8 fusion.7
  1.5 3.1 %collective-permute-start.2 = (s32[768]{0:T(1024)S(1)}, s32[768]{0:T(1024)S(1)}, u32[]{:S(2)}, u32[]{:S(2)}) collective-permute-start(s32[768]{0:T(1024)S(1)} %get-tuple-element.33), channel_id=1, source_target_pairs={{0,1},{1,0},{2,3},{3,2},{4,5},{5,4},{6,7},{7,6},{8,9},{9,8},{10,11... | collective-permute-start | bytes 9224 | tf_op jit(solution)/shard_map/ppermute | solution.py:317
  4.6 1.3 fusion.5
  5.9 0.0 collective-permute-start.3
  5.9 2.0 %collective-permute-start.1 = (bf16[768,768]{1,0:T(8,128)(2,1)}, bf16[768,768]{1,0:T(8,128)(2,1)S(1)}, u32[]{:S(2)}, u32[]{:S(2)}) collective-permute-start(bf16[768,768]{1,0:T(8,128)(2,1)} %bitcast.39), channel_id=1, source_target_pairs={{0,1},{1,0},{2,3},{3,2},{4,5},{5,4},{6,7},{7,6},{8,9},{9,8},{10,11... | collective-permute-start | bytes 3538952 | tf_op jit(solution)/shard_map/ppermute | solution.py:319
  7.9 2.5 %collective-permute-start = (bf16[768,768]{1,0:T(8,128)(2,1)}, bf16[768,768]{1,0:T(8,128)(2,1)}, u32[]{:S(2)}, u32[]{:S(2)}) collective-permute-start(bf16[768,768]{1,0:T(8,128)(2,1)} %bitcast.37), channel_id=1, source_target_pairs={{0,3},{1,2},{2,1},{3,0},{4,7},{5,6},{6,5},{7,4},{8,11},{9,10},{10,... | collective-permute-start | bytes 3538952 | tf_op jit(solution)/shard_map/ppermute | solution.py:320
  10.4 3.2 %multiply_reduce_fusion.3 = (f32[768]{0:T(1024)S(1)}, f32[768,1024]{1,0:T(8,128)S(1)}) fusion(bf16[768,1024]{1,0:T(8,128)(2,1)} %param.10, bf16[1,768,768]{2,1,0:T(8,128)(2,1)} %param.6), kind=kOutput, calls=%fused_computation.7 | convolution fusion | flops 1209531648 | bytes 5901312 | tf_op jit(solution)/shard_map/dot_general | solution.py:19
  13.6 1.5 multiply_reduce_fusion.2
  15.1 0.8 divide_convert_fusion.2
  16.0 2.8 %convolution_multiply_fusion.3.s00 = f32[768,768]{1,0:T(8,128)} fusion(bf16[768,1024]{1,0:T(8,128)(2,1)S(1)} %get-tuple-element.46.up0, bf16[768,1024]{1,0:T(8,128)(2,1)S(1)} %get-tuple-element.45.uc0), kind=kOutput, calls=%fused_computation.19 | convolution fusion | flops 1208549376 | bytes 5505024 | tf_op jit(solution)/shard_map/dot_general | solution.py:329
  18.8 0.9 sqrt.28.rp0
  19.7 0.9 sqrt.30.rc0
  20.6 1.0 copy.35.t00
  21.6 0.9 copy.36.t01
  22.6 0.9 copy.39.w0
  23.5 0.0 collective-permute-done.2
  23.5 0.9 broadcast_in_dim.46.t11
  24.4 0.9 broadcast_in_dim.45.t10
  25.4 0.0 collective-permute-done.3
  25.4 0.9 broadcast_in_dim.47.w1
  26.3 35.0 %collective-permute-done.fc1 = bf16[768,768]{1,0:T(8,128)(2,1)} collective-permute-done((bf16[768,768]{1,0:T(8,128)(2,1)}, bf16[768,768]{1,0:T(8,128)(2,1)}, u32[]{:S(2)}, u32[]{:S(2)}) %collective-permute-start) | collective-permute-done | bytes 1179680 | tf_op jit(solution)/shard_map/ppermute | solution.py:320
  61.2 2.7 %multiply_reduce_fusion.1 = (f32[768]{0:T(1024)S(1)}, f32[768,1024]{1,0:T(8,128)S(1)}) fusion(bf16[768,768]{1,0:T(8,128)(2,1)} %collective-permute-done.fc1, bf16[768,1024]{1,0:T(8,128)(2,1)S(1)} %copy-done), kind=kOutput, calls=%fused_computation.3 | convolution fusion | flops 1209531648 | bytes 5901312 | tf_op jit(solution)/shard_map/dot_general | solution.py:19
  64.0 0.0 collective-permute-done.1.fp1
  64.0 1.5 multiply_reduce_fusion
  65.5 0.4 divide_convert_fusion.up1
  65.9 1.0 copy-done.4
  66.9 1.4 convolution_multiply_fusion.1.s10
  68.3 0.0 copy-start.8
  68.4 0.4 divide_convert_fusion.1.uc1
  68.8 1.8 %copy-done.6 = bf16[768,1024]{1,0:T(8,128)(2,1)S(1)} copy-done((bf16[768,1024]{1,0:T(8,128)(2,1)S(1)}, bf16[768,1024]{1,0:T(8,128)(2,1)}, u32[]{:S(2)}) %copy-start.6) | copy-done | bytes 1572888
  70.6 1.4 convolution_multiply_fusion.2.s01
  72.1 0.8 copy-done.7
  72.8 4.7 %select_reduce_fusion = (f32[768]{0:T(1024)S(1)}, f32[768]{0:T(1024)S(1)}, f32[768]{0:T(1024)S(1)}, f32[768]{0:T(1024)S(1)}, f32[768]{0:T(1024)S(1)}, /*index=5*...) fusion(s32[768]{0:T(1024)S(1)} %get-tuple-element.47, s32[768]{0:T(1024)S(1)} %collective-permute-done.2, ...), kind=kOutput, calls=%fused_computation.8 | convolution fusion | flops 1220339712 | bytes 12619776 | tf_op jit(solution)/shard_map/dot_general | solution.py:329
  77.6 0.7 collective-permute-start.4
  78.3 0.6 multiply_reduce_fusion.4
  78.9 0.9 sqrt.31.rc1
  79.9 0.9 sqrt.29.rp1
  80.8 0.6 collective-permute-done.4
  81.4 1.0 copy.42.tot1
  82.3 0.9 copy.41.tot0
  83.3 0.6 multiply_reduce_fusion.5
  85.8 0.7 compare_select_fusion
  86.5 0.7 mul.57.stats_ref
  87.2 65.8 %backward.1 = (f32[96,256]{1,0:T(8,128)}, f32[96,256]{1,0:T(8,128)}, f32[8,128]{1,0:T(8,128)}) custom-call(f32[768,768]{1,0:T(8,128)} %convolution_multiply_fusion.3.s00, f32[768,768]{1,0:T(8,128)} %copy-done.9, f32[768,768]{1,0:T(8,128)} %copy-done.8, f32[768,768]{1,0:T(8,128)} %get-tuple-element.44.s11, s32[768,1]{1,0:T(8,128)} %copy.35.t00, ...), custom_call_target="tpu_custom_call" | custom-call | tf_op jit(solution)/shard_map/backward/pallas_call | solution.py:277
  153.0 1.4 fusion.6
  155.7 2.2 %broadcast_divide_fusion = f32[96,256]{1,0:T(8,128)} fusion(f32[96,256]{1,0:T(8,128)} %get-tuple-element.8, f32[]{:T(128)} %bitcast.8), kind=kLoop, calls=%fused_computation.20 | loop fusion | flops 24576 | bytes 196612 | tf_op jit(solution)/shard_map/div | solution.py:353
  157.9 2.2 %broadcast_divide_fusion.1 = f32[96,256]{1,0:T(8,128)} fusion(f32[96,256]{1,0:T(8,128)} %get-tuple-element.7, f32[]{:T(128)} %bitcast.8), kind=kLoop, calls=%fused_computation.21 | loop fusion | flops 24576 | bytes 196612 | tf_op jit(solution)/shard_map/div | solution.py:353
  (36 shorter events, 0.1 us)
Async XLA Ops:
  0.6 13.0 %copy-start = (bf16[768,1024]{1,0:T(8,128)(2,1)S(1)}, bf16[768,1024]{1,0:T(8,128)(2,1)}, u32[]{:S(2)}) copy-start(bf16[768,1024]{1,0:T(8,128)(2,1)} %param.11) | copy-start | bytes 4718596
  1.5 22.0 %collective-permute-start.2 = (s32[768]{0:T(1024)S(1)}, s32[768]{0:T(1024)S(1)}, u32[]{:S(2)}, u32[]{:S(2)}) collective-permute-start(s32[768]{0:T(1024)S(1)} %get-tuple-element.33), channel_id=1, source_target_pairs={{0,1},{1,0},{2,3},{3,2},{4,5},{5,4},{6,7},{7,6},{8,9},{9,8},{10,11... | collective-permute-start | bytes 9224 | tf_op jit(solution)/shard_map/ppermute | solution.py:317
  5.9 19.5 %collective-permute-start.3 = (f32[768]{0:T(1024)S(1)}, f32[768]{0:T(1024)S(1)}, u32[]{:S(2)}, u32[]{:S(2)}) collective-permute-start(f32[768]{0:T(1024)S(1)} %get-tuple-element.26), channel_id=1, source_target_pairs={{0,1},{1,0},{2,3},{3,2},{4,5},{5,4},{6,7},{7,6},{8,9},{9,8},{10,11... | collective-permute-start | bytes 9224 | tf_op jit(solution)/shard_map/ppermute | solution.py:318
  5.9 58.1 %collective-permute-start.1 = (bf16[768,768]{1,0:T(8,128)(2,1)}, bf16[768,768]{1,0:T(8,128)(2,1)S(1)}, u32[]{:S(2)}, u32[]{:S(2)}) collective-permute-start(bf16[768,768]{1,0:T(8,128)(2,1)} %bitcast.39), channel_id=1, source_target_pairs={{0,1},{1,0},{2,3},{3,2},{4,5},{5,4},{6,7},{7,6},{8,9},{9,8},{10,11... | collective-permute-start | bytes 3538952 | tf_op jit(solution)/shard_map/ppermute | solution.py:319
  7.9 5.7 %copy-start.10 = (bf16[1,768,768]{2,1,0:T(8,128)(2,1)S(1)}, bf16[1,768,768]{2,1,0:T(8,128)(2,1)}, u32[]{:S(2)}) copy-start(bf16[1,768,768]{2,1,0:T(8,128)(2,1)} %param.7) | copy-start | bytes 3538948
  7.9 53.3 %collective-permute-start = (bf16[768,768]{1,0:T(8,128)(2,1)}, bf16[768,768]{1,0:T(8,128)(2,1)}, u32[]{:S(2)}, u32[]{:S(2)}) collective-permute-start(bf16[768,768]{1,0:T(8,128)(2,1)} %bitcast.37), channel_id=1, source_target_pairs={{0,3},{1,2},{2,1},{3,0},{4,7},{5,6},{6,5},{7,4},{8,11},{9,10},{10,... | collective-permute-start | bytes 3538952 | tf_op jit(solution)/shard_map/ppermute | solution.py:320
  15.9 2.9 %copy-start.3 = (bf16[768,1024]{1,0:T(8,128)(2,1)}, bf16[768,1024]{1,0:T(8,128)(2,1)S(1)}, u32[]{:S(2)}) copy-start(bf16[768,1024]{1,0:T(8,128)(2,1)S(1)} %get-tuple-element.45.uc0) | copy-start | bytes 4718596
  16.0 2.9 %copy-start.5 = (bf16[768,1024]{1,0:T(8,128)(2,1)}, bf16[768,1024]{1,0:T(8,128)(2,1)S(1)}, u32[]{:S(2)}) copy-start(bf16[768,1024]{1,0:T(8,128)(2,1)S(1)} %get-tuple-element.46.up0) | copy-start | bytes 4718596
  18.8 3.7 %copy-start.12 = (f32[1,768]{1,0:T(1,128)S(1)}, f32[1,768]{1,0:T(1,128)}, u32[]{:S(2)}) copy-start(f32[1,768]{1,0:T(1,128)} %param.9) | copy-start | bytes 9220
  26.3 37.7 %copy-start.13 = (bf16[768,1024]{1,0:T(8,128)(2,1)S(1)}, bf16[768,1024]{1,0:T(8,128)(2,1)}, u32[]{:S(2)}) copy-start(bf16[768,1024]{1,0:T(8,128)(2,1)} %param.10) | copy-start | bytes 4718596
  64.0 1.5 copy-start.11
  65.5 1.4 copy-start.4
  66.9 5.2 %copy-start.1 = (bf16[768,1024]{1,0:T(8,128)(2,1)}, bf16[768,1024]{1,0:T(8,128)(2,1)S(1)}, u32[]{:S(2)}) copy-start(bf16[768,1024]{1,0:T(8,128)(2,1)S(1)} %divide_convert_fusion.up1) | copy-start | bytes 4718596
  68.3 3.7 %copy-start.8 = (f32[768,768]{1,0:T(8,128)}, f32[768,768]{1,0:T(8,128)S(1)}, u32[]{:S(2)}) copy-start(f32[768,768]{1,0:T(8,128)S(1)} %convolution_multiply_fusion.1.s10) | copy-start | bytes 7077892
  68.3 2.3 %copy-start.6 = (bf16[768,1024]{1,0:T(8,128)(2,1)S(1)}, bf16[768,1024]{1,0:T(8,128)(2,1)}, u32[]{:S(2)}) copy-start(bf16[768,1024]{1,0:T(8,128)(2,1)} %copy-done.5) | copy-start | bytes 4718596
  70.6 1.5 copy-start.2
  70.6 2.2 %copy-start.7 = (f32[768,768]{1,0:T(8,128)S(1)}, f32[768,768]{1,0:T(8,128)}, u32[]{:S(2)}) copy-start(f32[768,768]{1,0:T(8,128)} %convolution_multiply_fusion.3.s00) | copy-start | bytes 7077892
  72.0 5.5 %copy-start.9 = (f32[768,768]{1,0:T(8,128)}, f32[768,768]{1,0:T(8,128)S(1)}, u32[]{:S(2)}) copy-start(f32[768,768]{1,0:T(8,128)S(1)} %convolution_multiply_fusion.2.s01) | copy-start | bytes 7077892
  77.6 3.7 %collective-permute-start.4 = (f32[2,768]{1,0:T(2,128)S(1)}, f32[2,768]{1,0:T(2,128)S(1)}, u32[]{:S(2)}, u32[]{:S(2)}) collective-permute-start(f32[2,768]{1,0:T(2,128)S(1)} %pad_maximum_fusion), channel_id=1, source_target_pairs={{0,1},{1,0},{2,3},{3,2},{4,5},{5,4},{6,7},{7,6},{8,9},{9,8},{10,11... | collective-permute-start | bytes 18440 | tf_op jit(solution)/shard_map/ppermute | solution.py:339
where the time goes:
time: 162 us; the launch traced here: 161 us
  Pallas kernels  65.8 us (41%)
  waiting for transfers between devices  35.5 us (22%)
  matrix products  19.3 us (12%)
  local copies, waits for them, and re-layouts  16.8 us (10%)
  other arithmetic  10.2 us (6%)
  starting transfers between devices  8.26 us (5%)
  between operations  5.34 us (3%)
    pallas_call x1, Pallas kernels, backward(): pl.pallas_call(functools.partial(backward_kernel, nx, ny, nz), out_shape=...  65.8 us
    ppermute x1, waiting for transfers between devices, per_device(): far_c = lax.ppermute(own_c, 'blk', across)  35 us
    dot_general x4, matrix products, scores_of(): lax.dot_general(p[i][1], c[j][1], (((1,), (1,)), ((), ())), preferred_ele...  10.4 us
    dot_general x4, matrix products, embed_rows(): raw = jnp.dot(features, weight, preferred_element_type=F32)  8.9 us
    sqrt x4, local copies, waits for them, and re-layouts, embed_rows(): radius = jnp.sqrt(jnp.sum(raw * raw, axis=1, keepdims=True) + EPS)  3.65 us
    unnamed x28, local copies, waits for them, and re-layouts  3.63 us
  transfers between devices with their start and end apart: 5, of which 2 were waited for; matrix products, arithmetic and copies ran while one was open for 14% of the time, Pallas kernels for 0%

commit v1 on v0

--- a/solution.py
+++ b/solution.py
@@ -15,20 +15,13 @@
 BF16 = jnp.bfloat16
 
 
-def embed_rows(features, weight):
-    raw = jnp.dot(features, weight, preferred_element_type=F32)
-    radius = jnp.sqrt(jnp.sum(raw * raw, axis=1, keepdims=True) + EPS)
-    unit = raw / radius
-    return unit, unit.astype(BF16), radius
-
-
-def backward_kernel(
-    nx, ny, nz,
-    s00, s01, s10, s11, t00, t01, t10, t11, w0, w1, tot0, tot1, rp0, rp1, rc0, rc1,
-    up0, up1, uc0, uc1, fp0, fp1, fc0, fc1, stats_ref,
+def train_kernel(
+    nx, ny, nz, own_p, own_c, matched, row_weight, proj_p, proj_c,
     oa_ref, ob_ref, stats_out,
+    far_p, far_c, unit, radius, scores, part, pack, pack_in, lines, vecs,
     coeffs_t, high, low, head, core_in, first_out, first_in, own, second_out, second_in, last, last_in,
     stats_now, stats_in,
+    far_s, far_r, pack_s, pack_r,
     core_s, core_r, first_s, first_r, second_s, second_r, last_s, last_r, stats_s, stats_r,
 ):
     dp = lax.axis_index("dp")
@@ -82,8 +75,8 @@
             total = total + stats_in[axis, k]
         return total
 
-    rows, feat = fp0.shape
-    cols = up0.shape[1]
+    rows, feat = far_p.shape
+    cols = unit.shape[2]
     groups = nx * ny
     r = feat // (groups * 2)
     width = cols // nz
@@ -167,7 +160,7 @@
                 )
         return started
 
-    def finish(h, copies, out_ref):
+    def finish(h, copies, out_ref, weight_total):
         for q in range(2):
             p = 2 * h + q
             for copy in copies[q]:
@@ -175,15 +168,84 @@
             total = last[p, :, pl.ds(pl.multiple_of(z * half, half), half)]
             for m in range(nz - 1):
                 total = total + last_in[p, m]
-            out_ref[:, q * half:(q + 1) * half] = total
-
-    scores = ((s00, s01), (s10, s11))
-    relative = ((t00, t01), (t10, t11))
-    weights, totals = (w0, w1), (tot0, tot1)
-    radius_p, radius_c = (rp0, rp1), (rc0, rc1)
-    unit_p, unit_c = (up0, up1), (uc0, uc1)
-    feat_p, feat_c = (fp0, fp1), (fc0, fc1)
+            out_ref[:, q * half:(q + 1) * half] = total / weight_total
+
     step = 256
+    blocks = rows // step
+    local_feat = ((own_p.at[0], far_p), (own_c.at[0], far_c))
+    proj = (proj_p, proj_c)
+
+    beside = at(y, x, core, z + 1 - 2 * lax.rem(z, 2))
+    across = at(y, x, core, nz - 1 - z)
+    arrivals = [[], []]
+    for b in range(blocks):
+        for side, to in ((0, beside), (1, across)):
+            block = pl.ds(b * step, step)
+            arrivals[side].append(
+                send(local_feat[side][0].at[block, :], local_feat[side][1].at[block, :], far_s.at[side, b], far_r.at[side, b], to)
+            )
+
+    def embed(side, i, start):
+        block = pl.ds(start, step)
+        raw = jnp.dot(local_feat[side][i][block, :], proj[side][...], preferred_element_type=F32)
+        length = jnp.sqrt(jnp.sum(raw * raw, axis=1, keepdims=True) + EPS)
+        here = pl.ds(i * rows + start, step)
+        unit[side, here, :] = (raw / length).astype(BF16)
+        radius[side, here, :] = length
+
+    def score(i, p_start, j, c_start, c_count):
+        block = pl.ds(p_start, step)
+        value = LOGIT_SCALE * lax.dot_general(
+            unit[0, pl.ds(i * rows + p_start, step), :],
+            unit[1, pl.ds(j * rows + c_start, c_count), :],
+            (((1,), (1,)), ((), ())),
+            preferred_element_type=F32,
+        )
+        scores[i, j, block, pl.ds(c_start, c_count)] = value
+        part[i, block, :] = part[i, block, :] + jnp.sum(jnp.exp(value - LOGIT_SCALE), axis=1, keepdims=True)
+
+    def each_block(body):
+        def run(b, carry):
+            body(pl.multiple_of(b * step, step))
+            return carry
+
+        lax.fori_loop(0, blocks, run, 0)
+
+    part[...] = jnp.zeros_like(part)
+    lines[...] = jnp.zeros_like(lines)
+    each_block(lambda start: embed(0, 0, start))
+    each_block(lambda start: embed(1, 0, start))
+    each_block(lambda start: score(0, start, 0, 0, rows))
+    for b in range(blocks):
+        arrivals[0][b].wait()
+        embed(0, 1, b * step)
+        score(1, b * step, 0, 0, rows)
+        arrivals[1][b].wait()
+        embed(1, 1, b * step)
+        each_block(functools.partial(lambda c_start, start: score(0, start, 1, c_start, step), b * step))
+    each_block(lambda start: score(1, start, 1, 0, rows))
+
+    lane = lax.broadcasted_iota(jnp.int32, (rows, 128), 1)
+    turned_part = jnp.where(lane == 0, part[0], jnp.where(lane == 1, part[1], 0.0)).T
+    pack[...] = turned_part[0:8, :]
+    pack[2:3, :] = row_weight[...]
+    pack[3:4, :] = matched[...].astype(F32)
+    exchange = send(pack, pack_in, pack_s, pack_r, beside)
+    exchange.wait()
+    total_own = pack[0:1, :] + pack_in[1:2, :]
+    lines[0:1, :] = pack[2:3, :]
+    lines[1:2, :] = pack_in[2:3, :]
+    lines[2:3, :] = total_own
+    lines[3:4, :] = pack[1:2, :] + pack_in[0:1, :]
+    starts = ((z * rows).astype(F32), ((nz - 1 - z) * rows).astype(F32))
+    for j in range(2):
+        lines[4 + j:5 + j, :] = pack[3:4, :] - starts[j]
+        lines[6 + j:7 + j, :] = pack_in[3:4, :] - starts[j]
+    vecs[...] = lines[...].T
+    numbers = lax.broadcasted_iota(jnp.int32, (1, rows), 1).astype(F32)
+
+    def half_of(side, i):
+        return unit[side, i * rows:(i + 1) * rows, :]
 
     def directions(grad, unit, radius, where):
         grad = LOGIT_SCALE * grad
@@ -194,33 +256,35 @@
         low[where, :] = (direction - top.astype(F32)).astype(BF16)
 
     def prod_side(i):
-        def body(b, carry):
+        def body(b, matched_sum):
             start = pl.multiple_of(b * step, step)
             block = pl.ds(start, step)
+            here = pl.ds(i * rows + start, step)
+            weight = vecs[block, i:i + 1]
+            total = vecs[block, 2 + i:3 + i]
             grad = None
             for j in range(2):
-                probability = jnp.exp(scores[i][j][block, :] - LOGIT_SCALE) / totals[i][block, :]
-                match = relative[i][j][block, :] == lax.broadcasted_iota(jnp.int32, (step, rows), 1)
-                coeffs = (weights[i][block, :] * (probability - match.astype(F32))).astype(BF16)
+                value = scores[i, j, block, :]
+                match = vecs[block, 4 + 2 * i + j:5 + 2 * i + j] == numbers
+                matched_sum = matched_sum + weight * jnp.sum(jnp.where(match, value, 0.0), axis=1, keepdims=True)
+                probability = jnp.exp(value - LOGIT_SCALE) / total
+                coeffs = (weight * (probability - match.astype(F32))).astype(BF16)
                 coeffs_t[i, j * rows:(j + 1) * rows, block] = coeffs.T
-                term = jnp.dot(coeffs, unit_c[j][...], preferred_element_type=F32)
+                term = jnp.dot(coeffs, half_of(1, j), preferred_element_type=F32)
                 grad = term if grad is None else grad + term
-            directions(grad, unit_p[i][block, :], radius_p[i][block, :], pl.ds(i * rows + start, step))
-            return carry
-
-        lax.fori_loop(0, rows // step, body, 0)
+            directions(grad, unit[0, here, :], radius[0, here, :], here)
+            return matched_sum
+
+        return lax.fori_loop(0, blocks, body, jnp.zeros((step, 1), F32))
 
     def prec_side(j):
-        def body(b, carry):
-            start = pl.multiple_of(b * step, step)
-            block = pl.ds(start, step)
+        def body(start):
             here = pl.ds(j * rows + start, step)
-            grad = jnp.dot(coeffs_t[0, here, :], unit_p[0][...], preferred_element_type=F32)
-            grad = grad + jnp.dot(coeffs_t[1, here, :], unit_p[1][...], preferred_element_type=F32)
-            directions(grad, unit_c[j][block, :], radius_c[j][block, :], here)
-            return carry
-
-        lax.fori_loop(0, rows // step, body, 0)
+            grad = jnp.dot(coeffs_t[0, here, :], half_of(0, 0), preferred_element_type=F32)
+            grad = grad + jnp.dot(coeffs_t[1, here, :], half_of(0, 1), preferred_element_type=F32)
+            directions(grad, unit[1, here, :], radius[1, here, :], here)
+
+        each_block(body)
 
     def outer(h, features):
         def body(b, carry):
@@ -236,13 +300,15 @@
 
         lax.fori_loop(0, feat // step, body, 0)
 
-    stats_now[0] = stats_ref[...]
+    matched_sum = prod_side(0) + prod_side(1)
+    loss = jnp.sum(row_weight[...] * (LOGIT_SCALE + jnp.log(total_own)), axis=1, keepdims=True)
+    loss = loss - jnp.sum(matched_sum, axis=0, keepdims=True)
+    first_line = lax.broadcasted_iota(jnp.int32, (8, 128), 0) == 0
+    stats_now[0] = jnp.where(first_line, loss, jnp.sum(row_weight[...], axis=1, keepdims=True))
     small = stats_start(0)
-    prod_side(0)
-    prod_side(1)
+    outer(0, local_feat[0])
     stats_now[1] = stats_end(0, small)
     small = stats_start(1)
-    outer(0, feat_p)
     core_p = core_start(0)
     prec_side(0)
     first_p = first_start(0, core_p)
@@ -252,20 +318,23 @@
     second_p = second_start(0, first_p)
     stats_now[3] = stats_end(2, small)
     small = stats_start(3)
-    outer(1, feat_c)
+    outer(1, local_feat[1])
     core_c = core_start(1)
     last_p = last_start(0, second_p)
     first_c = first_start(1, core_c)
     second_c = second_start(1, first_c)
     last_c = last_start(1, second_c)
-    finish(0, last_p, oa_ref)
-    stats_out[...] = stats_end(3, small)
-    finish(1, last_c, ob_ref)
-
-
-def backward(nx, ny, nz, *operands):
-    feat = operands[-2].shape[1]
-    rows, cols = operands[16].shape
+    sums = stats_end(3, small)
+    weight_total = sums[1:2, 0:1]
+    stats_out[...] = sums / weight_total
+    finish(0, last_p, oa_ref, weight_total)
+    finish(1, last_c, ob_ref, weight_total)
+
+
+def train(nx, ny, nz, *operands):
+    rows, feat = operands[0].shape[1:]
+    cols = operands[-1].shape[1]
+    step = 256
     groups = nx * ny
     r = feat // (groups * 2)
     half = cols // nz // 2
@@ -275,11 +344,21 @@
     dma = pltpu.SemaphoreType.DMA
     vmem = pl.BlockSpec(memory_space=pltpu.VMEM)
     return pl.pallas_call(
-        functools.partial(backward_kernel, nx, ny, nz),
+        functools.partial(train_kernel, nx, ny, nz),
         out_shape=(out, out, jax.ShapeDtypeStruct((8, 128), F32)),
         in_specs=[vmem] * len(operands),
         out_specs=(vmem,) * 3,
         scratch_shapes=[
+            pltpu.VMEM((rows, feat), BF16),
+            pltpu.VMEM((rows, feat), BF16),
+            pltpu.VMEM((2, 2 * rows, cols), BF16),
+            pltpu.VMEM((2, 2 * rows, 1), F32),
+            pltpu.VMEM((2, 2, rows, rows), F32),
+            pltpu.VMEM((2, rows, 1), F32),
+            pltpu.VMEM((8, rows), F32),
+            pltpu.VMEM((8, rows), F32),
+            pltpu.VMEM((128, rows), F32),
+            pltpu.VMEM((rows, 128), F32),
             pltpu.VMEM((2, 2 * rows, rows), BF16),
             pltpu.VMEM((2 * rows, cols), BF16),
             pltpu.VMEM((2 * rows, cols), BF16),
@@ -294,6 +373,8 @@
             pltpu.VMEM((4, nz - 1, r, half), F32),
             pltpu.VMEM((4, 8, 128), F32),
             pltpu.VMEM((4, most, 8, 128), F32),
+            dma((2, rows // step)), dma((2, rows // step)),
+            dma, dma,
             dma((2, groups)), dma((2, groups)),
             dma((4, n - 1)), dma((4, n - 1)),
             dma((4, n - 1)), dma((4, n - 1)),
@@ -303,54 +384,13 @@
         compiler_params=pltpu.CompilerParams(
             collective_id=0, has_side_effects=True, vmem_limit_bytes=60 * 1024 * 1024
         ),
-        name="backward",
+        name="train",
     )(*operands)
 
 
-def per_device(nx, ny, prod_feat, prec_feat, matched, row_weight, proj_prod, proj_prec):
-    n = lax.axis_size("blk")
-    z = lax.axis_index("blk")
-    side = [(i, i ^ 1) for i in range(n)]
-    across = [(i, n - 1 - i) for i in range(n)]
-    own_p, own_c, own_t, own_w = prod_feat[0], prec_feat[0], matched[0], row_weight[0]
-    rows = own_p.shape[0]
-    far_t = lax.ppermute(own_t, "blk", side)
-    far_w = lax.ppermute(own_w, "blk", side)
-    far_p = lax.ppermute(own_p, "blk", side)
-    far_c = lax.ppermute(own_c, "blk", across)
-
-    feat_p, feat_c = (own_p, far_p), (own_c, far_c)
-    targets, weights = (own_t, far_t), (own_w, far_w)
-    p = [embed_rows(f, proj_prod) for f in feat_p]
-    c = [embed_rows(f, proj_prec) for f in feat_c]
-    starts = (z * rows, (n - 1 - z) * rows)
-
-    def scores_of(i, j):
-        return LOGIT_SCALE * lax.dot_general(
-            p[i][1], c[j][1], (((1,), (1,)), ((), ())), preferred_element_type=F32
-        )
-
-    scores = [[scores_of(i, j) for j in range(2)] for i in range(2)]
-    matches = [
-        [targets[i][:, None] == (starts[j] + lax.iota(jnp.int32, rows))[None, :] for j in range(2)] for i in range(2)
-    ]
-    part = [sum(jnp.sum(jnp.exp(scores[i][j] - LOGIT_SCALE), axis=1) for j in range(2)) for i in range(2)]
-    both = jnp.stack([part[1], part[0]])
-    both = lax.ppermute(both, "blk", side)
-    totals = [part[0] + both[0], part[1] + both[1]]
-    positive = [sum(jnp.sum(jnp.where(matches[i][j], scores[i][j], 0.0), axis=1) for j in range(2)) for i in range(2)]
-    loss_local = (
-        jnp.sum(own_w * (LOGIT_SCALE + jnp.log(totals[0]))) - jnp.sum(own_w * positive[0]) - jnp.sum(far_w * positive[1])
-    )
-    stats = jnp.where(lax.iota(jnp.int32, 8)[:, None] == 0, loss_local, jnp.sum(own_w)) * jnp.ones((8, 128), F32)
-    relative = [(targets[i] - starts[j])[:, None] for i in range(2) for j in range(2)]
-    sum_p, sum_c, stats = backward(
-        nx, ny, n,
-        *scores[0], *scores[1], *relative, *(w[:, None] for w in weights), *(t[:, None] for t in totals),
-        p[0][2], p[1][2], c[0][2], c[1][2], p[0][1], p[1][1], c[0][1], c[1][1], *feat_p, *feat_c, stats,
-    )
-    weight_total = stats[1, 0]
-    return (stats[0, 0] / weight_total, sum_p / weight_total, sum_c / weight_total)
+def per_device(nx, ny, *operands):
+    sum_p, sum_c, stats = train(nx, ny, lax.axis_size("blk"), *operands)
+    return (stats[0, 0], sum_p, sum_c)
 
 
 def solution(mesh):

time: 162 us -> 129 us (0.80)
  Pallas kernels: 65.8 us -> 124 us
  waiting for transfers between devices: 35.5 us -> 0 us
  matrix products: 19.3 us -> 0 us
  local copies, waits for them, and re-layouts: 16.8 us -> 4.26 us
  other arithmetic: 10.2 us -> 0 us
  starting transfers between devices: 8.26 us -> 0 us
  between operations: 5.34 us -> 0.64 us
    pallas_call x1, Pallas kernels: 65.8 us -> 124 us  [train(): pl.pallas_call(functools.partial(train_kernel, nx, ny, nz), out_shape=(ou...]
    ppermute x5 -> x0, waiting for transfers between devices: 35.5 us -> none  [the longest x1 35 us: per_device(): far_c = lax.ppermute(own_c, 'blk', across)]
    dot_general x8 -> x0, matrix products: 19.3 us -> none  [the longest x4 10.4 us: scores_of(): lax.dot_general(p[i][1], c[j][1], (((1,), (1,)), ((), ())), preferred_ele...]
    ppermute x5 -> x0, starting transfers between devices: 8.26 us -> none  [the longest x1 3.09 us: per_device(): far_t = lax.ppermute(own_t, 'blk', side)]
    div x2 -> x0, other arithmetic: 4.47 us -> none  [the longest x1 2.24 us: per_device(): sum_c / weight_total]
    sqrt x4 -> x0, local copies, waits for them, and re-layouts: 3.65 us -> none  [embed_rows(): radius = jnp.sqrt(jnp.sum(raw * raw, axis=1, keepdims=True) + EPS)]
    broadcast_in_dim x3 -> x0, local copies, waits for them, and re-layouts: 2.75 us -> none  [the longest x2 1.84 us: per_device(): (targets[i] - starts[j])[:, None]]
    reduce_sum x3 -> x0, other arithmetic: 2.53 us -> none  [the longest x1 1.3 us: per_device(): jnp.sum(own_w)]
  transfers between devices with their start and end apart: 5 -> 0, of which waited for: 2 -> 0; matrix products, arithmetic and copies ran while one was open for 14% -> 0% of each run, Pallas kernels for 0% -> 0%
where the time goes in v1:
time: 129 us; the launch traced here: 128 us
  Pallas kernels  124 us (96%)
  local copies, waits for them, and re-layouts  4.26 us (3%)
    pallas_call x1, Pallas kernels, train(): pl.pallas_call(functools.partial(train_kernel, nx, ny, nz), out_shape=(ou...  124 us
    unnamed x2, local copies, waits for them, and re-layouts  3.08 us

profile of v1, /device:TPU:0, one launch (start us, length us, event | category | flops | bytes accessed | tf_op | source)
XLA Modules:
  0.0 128.5 jit_solution(653045893316784034)
XLA Ops:
  0.6 123.6 %train.1 = (f32[96,256]{1,0:T(8,128)}, f32[96,256]{1,0:T(8,128)}, f32[8,128]{1,0:T(8,128)}) custom-call(bf16[1,768,768]{2,1,0:T(8,128)(2,1)} %own_p.1, bf16[1,768,768]{2,1,0:T(8,128)(2,1)} %own_c.1, s32[1,768]{1,0:T(1,128)} %matched.1, f32[1,768]{1,0:T(1,128)} %row_weight.1, bf16[768,1024]{1,0:T(8,128)(2,1)} %proj_p.1, bf16[768,1024]{1,0:T(8,128)(2,1)} %proj_c.1), custom_call_target="tpu_custom_call" | custom-call | tf_op jit(solution)/shard_map/train/pallas_call | solution.py:346
  124.2 1.2 slice.3
  125.4 1.5 %copy.11 = f32[96,256]{1,0:T(8,128)} copy(f32[96,256]{1,0:T(8,128)} %get-tuple-element.13) | data formatting | bytes 196608
  126.9 1.5 %copy.12 = f32[96,256]{1,0:T(8,128)} copy(f32[96,256]{1,0:T(8,128)} %get-tuple-element.14) | data formatting | bytes 196608

commit v2 on v1

--- a/solution.py
+++ b/solution.py
@@ -18,8 +18,8 @@
 def train_kernel(
     nx, ny, nz, own_p, own_c, matched, row_weight, proj_p, proj_c,
     oa_ref, ob_ref, stats_out,
-    far_p, far_c, unit, radius, scores, part, pack, pack_in, lines, vecs,
-    coeffs_t, high, low, head, core_in, first_out, first_in, own, second_out, second_in, last, last_in,
+    far_p, far_c, unit, shrink, scores, part, pack, pack_in, lines, vecs,
+    coeffs_t, turns, head, core_in, first_out, first_in, own, second_out, second_in, last, last_in,
     stats_now, stats_in,
     far_s, far_r, pack_s, pack_r,
     core_s, core_r, first_s, first_r, second_s, second_r, last_s, last_r, stats_s, stats_r,
@@ -88,12 +88,6 @@
 
     def head_rows(g, cc):
         return pl.ds(pl.multiple_of((g * 2 + cc) * r, 8), r)
-
-    def core_start(h):
-        return [
-            send(head.at[h, head_rows(g, 1 - core)], core_in.at[h, g], core_s.at[h, g], core_r.at[h, g], twin)
-            for g in range(groups)
-        ]
 
     def place(q, i1, i2):
         return i2 * nx + i1 if q == 0 else i1 * nx + i2
@@ -190,8 +184,9 @@
         raw = jnp.dot(local_feat[side][i][block, :], proj[side][...], preferred_element_type=F32)
         length = jnp.sqrt(jnp.sum(raw * raw, axis=1, keepdims=True) + EPS)
         here = pl.ds(i * rows + start, step)
-        unit[side, here, :] = (raw / length).astype(BF16)
-        radius[side, here, :] = length
+        inverse = 1.0 / length
+        unit[side, here, :] = (raw * inverse).astype(BF16)
+        shrink[side, here, :] = LOGIT_SCALE * inverse
 
     def score(i, p_start, j, c_start, c_count):
         block = pl.ds(p_start, step)
@@ -220,10 +215,13 @@
         arrivals[0][b].wait()
         embed(0, 1, b * step)
         score(1, b * step, 0, 0, rows)
+        for done in range(b):
+            score(1, b * step, 1, done * step, step)
         arrivals[1][b].wait()
         embed(1, 1, b * step)
         each_block(functools.partial(lambda c_start, start: score(0, start, 1, c_start, step), b * step))
-    each_block(lambda start: score(1, start, 1, 0, rows))
+        for done in range(b + 1):
+            score(1, done * step, 1, b * step, step)
 
     lane = lax.broadcasted_iota(jnp.int32, (rows, 128), 1)
     turned_part = jnp.where(lane == 0, part[0], jnp.where(lane == 1, part[1], 0.0)).T
@@ -247,13 +245,10 @@
     def half_of(side, i):
         return unit[side, i * rows:(i + 1) * rows, :]
 
-    def directions(grad, unit, radius, where):
-        grad = LOGIT_SCALE * grad
-        unit = unit.astype(F32)
-        direction = (grad - unit * jnp.sum(unit * grad, axis=1, keepdims=True)) / radius
-        top = direction.astype(BF16)
-        high[where, :] = top
-        low[where, :] = (direction - top.astype(F32)).astype(BF16)
+    def directions(grad, unit16, scale, where):
+        wide = unit16.astype(F32)
+        across_unit = grad - wide * jnp.sum(wide * grad, axis=1, keepdims=True)
+        turns[where, :] = (across_unit * scale).astype(BF16)
 
     def prod_side(i):
         def body(b, matched_sum):
@@ -261,44 +256,49 @@
             block = pl.ds(start, step)
             here = pl.ds(i * rows + start, step)
             weight = vecs[block, i:i + 1]
-            total = vecs[block, 2 + i:3 + i]
+            inverse = 1.0 / vecs[block, 2 + i:3 + i]
             grad = None
             for j in range(2):
                 value = scores[i, j, block, :]
                 match = vecs[block, 4 + 2 * i + j:5 + 2 * i + j] == numbers
                 matched_sum = matched_sum + weight * jnp.sum(jnp.where(match, value, 0.0), axis=1, keepdims=True)
-                probability = jnp.exp(value - LOGIT_SCALE) / total
+                probability = jnp.exp(value - LOGIT_SCALE) * inverse
                 coeffs = (weight * (probability - match.astype(F32))).astype(BF16)
                 coeffs_t[i, j * rows:(j + 1) * rows, block] = coeffs.T
                 term = jnp.dot(coeffs, half_of(1, j), preferred_element_type=F32)
                 grad = term if grad is None else grad + term
-            directions(grad, unit[0, here, :], radius[0, here, :], here)
+            directions(grad, unit[0, here, :], shrink[0, here, :], here)
             return matched_sum
 
         return lax.fori_loop(0, blocks, body, jnp.zeros((step, 1), F32))
 
-    def prec_side(j):
-        def body(start):
-            here = pl.ds(j * rows + start, step)
+    def prec_side(first, count):
+        def body(b, carry):
+            here = pl.ds(pl.multiple_of(b * step, step), step)
             grad = jnp.dot(coeffs_t[0, here, :], half_of(0, 0), preferred_element_type=F32)
             grad = grad + jnp.dot(coeffs_t[1, here, :], half_of(0, 1), preferred_element_type=F32)
-            directions(grad, unit[1, here, :], radius[1, here, :], here)
-
-        each_block(body)
+            directions(grad, unit[1, here, :], shrink[1, here, :], here)
+            return carry
+
+        lax.fori_loop(first, first + count, body, 0)
 
     def outer(h, features):
-        def body(b, carry):
-            block = pl.ds(pl.multiple_of(b * step, step), step)
+        copies = []
+        for b in range(feat // step):
+            block = slice(b * step, (b + 1) * step)
             total = None
             for i in range(2):
-                turned = features[i][:, block].T
-                for term in (high, low):
-                    product = jnp.dot(turned, term[i * rows:(i + 1) * rows, :], preferred_element_type=F32)
-                    total = product if total is None else total + product
+                product = jnp.dot(
+                    features[i][:, block].T, turns[i * rows:(i + 1) * rows, :], preferred_element_type=F32
+                )
+                total = product if total is None else total + product
             head[h, block, :] = total
-            return carry
-
-        lax.fori_loop(0, feat // step, body, 0)
+            while len(copies) < groups and (len(copies) + 1) * 2 * r <= (b + 1) * step:
+                g = len(copies)
+                copies.append(
+                    send(head.at[h, head_rows(g, 1 - core)], core_in.at[h, g], core_s.at[h, g], core_r.at[h, g], twin)
+                )
+        return copies
 
     matched_sum = prod_side(0) + prod_side(1)
     loss = jnp.sum(row_weight[...] * (LOGIT_SCALE + jnp.log(total_own)), axis=1, keepdims=True)
@@ -306,21 +306,21 @@
     first_line = lax.broadcasted_iota(jnp.int32, (8, 128), 0) == 0
     stats_now[0] = jnp.where(first_line, loss, jnp.sum(row_weight[...], axis=1, keepdims=True))
     small = stats_start(0)
-    outer(0, local_feat[0])
+    core_p = outer(0, local_feat[0])
     stats_now[1] = stats_end(0, small)
     small = stats_start(1)
-    core_p = core_start(0)
-    prec_side(0)
+    third = 2 * blocks // 3
+    prec_side(0, third)
     first_p = first_start(0, core_p)
     stats_now[2] = stats_end(1, small)
     small = stats_start(2)
-    prec_side(1)
+    prec_side(third, third)
     second_p = second_start(0, first_p)
     stats_now[3] = stats_end(2, small)
     small = stats_start(3)
-    outer(1, local_feat[1])
-    core_c = core_start(1)
+    prec_side(2 * third, 2 * blocks - 2 * third)
     last_p = last_start(0, second_p)
+    core_c = outer(1, local_feat[1])
     first_c = first_start(1, core_c)
     second_c = second_start(1, first_c)
     last_c = last_start(1, second_c)
@@ -361,7 +361,6 @@
             pltpu.VMEM((rows, 128), F32),
             pltpu.VMEM((2, 2 * rows, rows), BF16),
             pltpu.VMEM((2 * rows, cols), BF16),
-            pltpu.VMEM((2 * rows, cols), BF16),
             pltpu.VMEM((2, feat, cols), F32),
             pltpu.VMEM((2, groups, r, cols), F32),
             pltpu.VMEM((4, n - 1, n, r, cols // 2), BF16),

time: 129 us -> 123 us (0.953)
  Pallas kernels: 124 us -> 118 us
    pallas_call x1, Pallas kernels: 124 us -> 118 us  [train(): pl.pallas_call(functools.partial(train_kernel, nx, ny, nz), out_shape=(ou...]
where the time goes in v2:
time: 123 us
  Pallas kernels  118 us (96%)
  local copies, waits for them, and re-layouts  4.26 us (3%)
    pallas_call x1, Pallas kernels, train(): pl.pallas_call(functools.partial(train_kernel, nx, ny, nz), out_shape=(ou...  118 us
    unnamed x2, local copies, waits for them, and re-layouts  3.08 us

profile of v2, /device:TPU:0, one launch (start us, length us, event | category | flops | bytes accessed | tf_op | source)
XLA Modules:
  0.0 122.8 jit_solution(10705583531559686260)
XLA Ops:
  0.6 117.9 %train.1 = (f32[96,256]{1,0:T(8,128)}, f32[96,256]{1,0:T(8,128)}, f32[8,128]{1,0:T(8,128)}) custom-call(bf16[1,768,768]{2,1,0:T(8,128)(2,1)} %own_p.1, bf16[1,768,768]{2,1,0:T(8,128)(2,1)} %own_c.1, s32[1,768]{1,0:T(1,128)} %matched.1, f32[1,768]{1,0:T(1,128)} %row_weight.1, bf16[768,1024]{1,0:T(8,128)(2,1)} %proj_p.1, bf16[768,1024]{1,0:T(8,128)(2,1)} %proj_c.1), custom_call_target="tpu_custom_call" | custom-call | tf_op jit(solution)/shard_map/train/pallas_call | solution.py:346
  118.6 1.2 slice.3
  119.8 1.5 %copy.11 = f32[96,256]{1,0:T(8,128)} copy(f32[96,256]{1,0:T(8,128)} %get-tuple-element.13) | data formatting | bytes 196608
  121.3 1.5 %copy.12 = f32[96,256]{1,0:T(8,128)} copy(f32[96,256]{1,0:T(8,128)} %get-tuple-element.14) | data formatting | bytes 196608
